TPU v7x, 256 devices: a whole 4x4x8 slice. The times are simulated.
256 devices in a mesh: ra: 16 (over x, z_hi, core), rb: 16 (over y, z_lo).
Axes of the slice: x: 4, y: 4, z: 8 (z_hi: 2, z_lo: 4; z = z_hi * 4 + z_lo), core: 2. Of those that a mesh axis runs over, the one named last changes fastest.
Arguments:
- features_a: bfloat16 [32, 128, 1024], P('ra', 'rb'), may hold values from -600 to 600
- features_b: bfloat16 [32, 128, 1024], P('rb', 'ra'), may hold values from -600 to 600
- weight_one: bfloat16 [16, 81], replicated, may hold values from -16 to 16
- bias_one: float32 [16], replicated, may hold values from -3 to 3
- weight_two: bfloat16 [16, 81], replicated, may hold values from -0.25 to 0.25
- bias_two: float32 [1], replicated, may hold values from -3 to 3
Outputs:
- consensus: float32 [32, 128, 32, 128], P('ra', None, 'rb')
All inputs are finite; a program needn't handle non-finite values.
Results may differ from a plain program's by a relative error of at most 0.0053.
Values may be sent and summed in bfloat16 or wider, within the bound.
A program may use at most 192 MiB of HBM per device.

v0:
```python
import jax
import jax.numpy as jnp
from jax import lax
from jax.sharding import PartitionSpec as P


def extended(cells, sides, width):
    for axis, dim in sides:
        count = lax.axis_size(axis)
        ends = count - 1
        head = lax.slice_in_dim(cells, 0, width, axis=dim)
        tail = lax.slice_in_dim(cells, cells.shape[dim] - width, cells.shape[dim], axis=dim)
        cells = jnp.concatenate(
            [
                lax.ppermute(tail, axis, [(i, (i + 1) % count) for i in range(ends)]),
                cells,
                lax.ppermute(head, axis, [((i + 1) % count, i) for i in range(ends)]),
            ],
            axis=dim,
        )
    return cells


def normalize(features):
    values = features.astype(jnp.float32)
    scale = lax.rsqrt(jnp.sum(values * values, axis=-1, keepdims=True) + 1e-06)
    return (values * scale).astype(jnp.bfloat16)


def correlate(norm_a, norm_b):
    gathered = lax.all_gather(norm_a, "rb", axis=1, tiled=True)
    channels = gathered.shape[2]
    flat_a = gathered.reshape(-1, channels)
    piece = lax.all_gather(norm_b, "ra", axis=1, tiled=True)
    product = lax.dot_general(
        flat_a,
        piece.reshape(-1, channels),
        (((1,), (1,)), ((), ())),
        preferred_element_type=jnp.float32,
    )
    return product.reshape(
        gathered.shape[0], gathered.shape[1], piece.shape[0], piece.shape[1]
    ).astype(jnp.bfloat16)


def pad_columns(volume):
    return jnp.pad(volume, ((0, 0), (1, 1), (0, 0), (1, 1)))


def first_layer(volume, weight_one, bias_one, out_rows, out_k):
    width_j = volume.shape[1] - 2
    width_l = volume.shape[3] - 2

    def first_one_row(row_start):
        block = lax.dynamic_slice_in_dim(volume, row_start, 3, 0)
        patches = jnp.stack(
            [
                block[t_i, t_j : t_j + width_j, t_k : t_k + out_k, t_l : t_l + width_l]
                for t_i in range(3)
                for t_j in range(3)
                for t_k in range(3)
                for t_l in range(3)
            ]
        )
        before = lax.dot_general(
            weight_one, patches, (((1,), (0,)), ((), ())), preferred_element_type=jnp.float32
        )
        return jax.nn.relu(before + bias_one[:, None, None, None])

    return lax.map(first_one_row, jnp.arange(out_rows, dtype=jnp.int32))


def second_sums(hidden_pad, weight_two, out_rows, out_k):
    width_j = hidden_pad.shape[2] - 2
    width_l = hidden_pad.shape[4] - 2

    def second_one_row(row_start):
        total = jnp.zeros((width_j, out_k, width_l), jnp.float32)
        for t_i in range(3):
            plane = lax.dynamic_index_in_dim(hidden_pad, row_start + t_i, 0, keepdims=False)
            taps = lax.dot_general(
                weight_two[:, 27 * t_i : 27 * t_i + 27],
                plane,
                (((0,), (0,)), ((), ())),
                preferred_element_type=jnp.float32,
            )
            for t_j in range(3):
                for t_k in range(3):
                    for t_l in range(3):
                        total = (
                            total
                            + taps[
                                9 * t_j + 3 * t_k + t_l,
                                t_j : t_j + width_j,
                                t_k : t_k + out_k,
                                t_l : t_l + width_l,
                            ]
                        )
        return total

    return lax.map(second_one_row, jnp.arange(out_rows, dtype=jnp.int32))


def second_layer(hidden_pad, weight_two, bias_two, out_rows, out_k):
    return jax.nn.relu(second_sums(hidden_pad, weight_two, out_rows, out_k) + bias_two[0])


def per_device(features_a, features_b, weight_one, bias_one, weight_two, bias_two):
    norm_a = normalize(features_a)
    norm_b = normalize(features_b)
    rows_a = norm_a.shape[0]
    rows_b = norm_b.shape[0]
    volume = correlate(norm_a, norm_b)
    padded = extended(volume, (("ra", 0), ("rb", 2)), 1)
    hidden = first_layer(pad_columns(padded), weight_one, bias_one, rows_a, rows_b).astype(
        jnp.bfloat16
    )
    hidden = extended(hidden, (("ra", 0), ("rb", 3)), 1)
    hidden = jnp.pad(hidden, ((0, 0), (0, 0), (1, 1), (0, 0), (1, 1)))
    return second_layer(hidden, weight_two, bias_two, rows_a, rows_b)


def solution(mesh):
    return jax.shard_map(
        per_device,
        mesh=mesh,
        in_specs=(P("ra", "rb", None), P("rb", "ra", None), P(), P(), P(), P()),
        out_specs=P("ra", None, "rb", None),
        check_vma=False,
    )
```

profile of v0, /device:TPU:232, one launch (start us, length us, event | category | flops | bytes accessed | tf_op | source)
XLA Modules:
  0.0 701.4 jit_solution(13057398529258511894)
XLA Ops:
  1.7 36.8 %all_gather.6 = bf16[2,128,1024]{2,1,0:T(8,128)(2,1)S(1)} all-gather(bf16[2,8,1024]{2,1,0:T(8,128)(2,1)S(1)} %fusion.41), channel_id=1, replica_groups=mesh['ra'=16,'rb'=16] {'rb'}, dimensions={1}, use_global_device_ids=true | all-gather | bytes 557056 | tf_op jit(solution)/shard_map/all_gather | solution.py:31
  40.2 27.3 %all_gather.7 = bf16[2,128,1024]{2,1,0:T(8,128)(2,1)S(1)} all-gather(bf16[2,8,1024]{2,1,0:T(8,128)(2,1)S(1)} %fusion.43), channel_id=1, replica_groups=mesh['ra'=16,'rb'=16] {'ra'}, dimensions={1}, use_global_device_ids=true | all-gather | bytes 557056 | tf_op jit(solution)/shard_map/all_gather | solution.py:34
  67.9 2.3 collective-permute-start
  70.2 9.7 %collective-permute-start.1 = (bf16[1,128,2,128]{3,1,2,0:T(8,128)(2,1)S(1)}, bf16[1,128,2,128]{3,1,2,0:T(8,128)(2,1)S(1)}, u32[]{:S(2)}, u32[]{:S(2)}) collective-permute-start(bf16[1,128,2,128]{3,1,2,0:T(8,128)(2,1)S(1)} %get-tuple-element.226), channel_id=1, source_target_pairs={{16,0},{32,16},{48,32},{64,48},{80,64},{96,80},{112,96},{128,112},... | collective-permute-start | bytes 196616 | tf_op jit(solution)/shard_map/ppermute | solution.py:17
  81.8 5.7 collective-permute-start.2
  87.5 1.9 collective-permute-start.3
  90.6 7.8 %collective-permute-done.3 = bf16[4,128,1,128]{3,1,2,0:T(8,128)(2,1)} collective-permute-done((bf16[4,128,1,128]{3,1,2,0:T(8,128)(2,1)S(1)}, bf16[4,128,1,128]{3,1,2,0:T(8,128)(2,1)}, u32[]{:S(2)}, u32[]{:S(2)}) %collective-permute-start.3) | collective-permute-done | bytes 131104 | tf_op jit(solution)/shard_map/ppermute | solution.py:17
  100.3 225.3 %while.24 = (s32[]{:T(128)}, bf16[2,16,128,2,128]{4,1,3,2,0:T(8,128)(2,1)S(1)}, s32[2]{0:T(128)S(1)}, bf16[4,130,4,130]{3,1,2,0:T(8,128)(2,1)S(1)}, bf16[16,81]{1,0:T(8,128)(2,1)S(1)}, /*index=5*/f32[16]{0:T(128)S(1)}) while((s32[]{:T(128)}, bf16[2,16,128,2,128]{4,1,3,2,0:T(8,128)(2,1)S(1)}, s32[2]{0:T(128)S(1)}, ...), condition=%wide.region_3.4_spmd.clone, body=%wide.region_2.3_spmd.sunk.clone | while | flops 85983240 | bytes 39260856 | solution.py:70
  102.8 4.8 fusion.70
  167.6 41.6 %stack.5 = bf16[81,128,2,128]{3,0,2,1:T(8,128)(2,1)} concatenate(bf16[1,128,2,128]{3,0,2,1:T(2,128)(2,1)S(1)} %copy.263, bf16[1,128,2,128]{3,0,2,1:T(2,128)(2,1)S(1)} %copy.264, bf16[1,128,2,128]{3,0,2,1:T(2,128)(2,1)} %copy.265, bf16[1,128,2,128]{3,0,2,1:T(2,128)(2,1)} %copy.266, bf16[1,128,2,128]{3,0,2,1:T(2,128)(2,1)} %copy.267, bf16[1,128,2,128]{3,0,2,1:T(2,128)(2,1)} %copy.268, ...), dimensions={0} | concatenate | bytes 10616832 | tf_op jit(solution)/shard_map/while/body/eval_jaxpr/stack | solution.py:56
  209.2 3.7 bitcast_dynamic-update-slice_fusion.3
  215.4 4.8 fusion.70
  280.2 41.6 %stack.5 = bf16[81,128,2,128]{3,0,2,1:T(8,128)(2,1)} concatenate(bf16[1,128,2,128]{3,0,2,1:T(2,128)(2,1)S(1)} %copy.263, bf16[1,128,2,128]{3,0,2,1:T(2,128)(2,1)S(1)} %copy.264, bf16[1,128,2,128]{3,0,2,1:T(2,128)(2,1)} %copy.265, bf16[1,128,2,128]{3,0,2,1:T(2,128)(2,1)} %copy.266, bf16[1,128,2,128]{3,0,2,1:T(2,128)(2,1)} %copy.267, bf16[1,128,2,128]{3,0,2,1:T(2,128)(2,1)} %copy.268, ...), dimensions={0} | concatenate | bytes 10616832 | tf_op jit(solution)/shard_map/while/body/eval_jaxpr/stack | solution.py:56
  321.7 3.7 bitcast_dynamic-update-slice_fusion.3
  326.0 3.7 collective-permute-start.4
  329.8 5.7 collective-permute-start.5
  335.5 28.8 %collective-permute-done.4 = bf16[1,16,128,2,128]{4,1,3,2,0:T(8,128)(2,1)S(1)} collective-permute-done((bf16[1,16,128,2,128]{4,1,3,2,0:T(8,128)(2,1)S(1)}, bf16[1,16,128,2,128]{4,1,3,2,0:T(8,128)(2,1)S(1)}, u32[]{:S(2)}, u32[]{:S(2)}) %collective-permute-start.4) | collective-permute-done | bytes 1048608 | tf_op jit(solution)/shard_map/ppermute | solution.py:15
  365.8 2.7 fusion.45
  368.5 4.9 collective-permute-start.6
  373.5 9.9 %collective-permute-start.7 = (bf16[4,16,128,1,128]{4,1,3,2,0:T(8,128)(2,1)}, bf16[4,16,128,1,128]{4,1,3,2,0:T(8,128)(2,1)}, u32[]{:S(2)}, u32[]{:S(2)}) collective-permute-start(bf16[4,16,128,1,128]{4,1,3,2,0:T(8,128)(2,1)} %get-tuple-element.220), channel_id=1, source_target_pairs={{1,0},{2,1},{3,2},{4,3},{5,4},{6,5},{7,6},{8,7},{9,8},{10,9},{11,1... | collective-permute-start | bytes 6291464 | tf_op jit(solution)/shard_map/ppermute | solution.py:17
  384.0 39.5 %collective-permute-done.6 = bf16[4,16,128,1,128]{4,1,3,2,0:T(8,128)(2,1)} collective-permute-done((bf16[4,16,128,1,128]{4,1,3,2,0:T(8,128)(2,1)}, bf16[4,16,128,1,128]{4,1,3,2,0:T(8,128)(2,1)}, u32[]{:S(2)}, u32[]{:S(2)}) %collective-permute-start.6) | collective-permute-done | bytes 2097184 | tf_op jit(solution)/shard_map/ppermute | solution.py:15
  423.5 86.5 %collective-permute-done.7 = bf16[4,16,128,1,128]{4,1,3,2,0:T(8,128)(2,1)} collective-permute-done((bf16[4,16,128,1,128]{4,1,3,2,0:T(8,128)(2,1)}, bf16[4,16,128,1,128]{4,1,3,2,0:T(8,128)(2,1)}, u32[]{:S(2)}, u32[]{:S(2)}) %collective-permute-start.7) | collective-permute-done | bytes 2097184 | tf_op jit(solution)/shard_map/ppermute | solution.py:17
  510.0 22.6 %select_maximum_fusion = bf16[4,16,130,4,130]{4,1,3,2,0:T(8,128)(2,1)} fusion(bf16[4,16,128,1,128]{4,1,3,2,0:T(8,128)(2,1)} %collective-permute-done.7, bf16[4,16,128,1,128]{4,1,3,2,0:T(8,128)(2,1)} %collective-permute-done.6, bf16[1,16,128,2,128]{4,1,3,2,0:T(8,128)(2,1)} %copy-done, bf16[2,16,128,2,128]{4,1,3,2,0:T(8,128)(2,1)S(1)} %get-tuple-element.103, ...), kind=kLoop, calls=%fused_computation.165 | loop fusion | flops 116812800 | bytes 17041408 | tf_op jit(solution)/shard_map/concatenate | solution.py:13
  532.6 168.0 %while.25 = (s32[]{:T(128)}, f32[2,128,2,128]{3,2,1,0:T(2,128)S(1)}, s32[2]{0:T(128)S(1)}, bf16[4,16,130,4,130]{4,1,3,2,0:T(8,128)(2,1)}, bf16[16,81]{1,0:T(8,128)(2,1)S(1)}) while((s32[]{:T(128)}, f32[2,128,2,128]{3,2,1,0:T(2,128)S(1)}, s32[2]{0:T(128)S(1)}, bf16[4,16,130,4,130]{4,1,3,2,0:T(8,128)(2,1)}, ...), condition=%wide.region_5.6_spmd.clone, body=%wide.region_4.5_spmd.sunk.clone | while | flops 177840640 | bytes 45699956 | solution.py:101
  534.5 10.6 %convolution_bitcast_fusion.10 = f32[27,130,4,130]{3,0,2,1:T(8,128)} fusion(bf16[4,16,130,4,130]{4,1,3,2,0:T(8,128)(2,1)} %get-tuple-element.604, s32[]{:T(128)S(6)} %select_n.32, bf16[16,81]{1,0:T(8,128)(2,1)S(1)} %get-tuple-element.605), kind=kOutput, calls=%fused_computation.60.clone.1.clone | convolution fusion | flops 58406400 | bytes 11563236 | tf_op jit(solution)/shard_map/while/body/eval_jaxpr/dot_general | solution.py:81
  546.4 10.5 %convolution_bitcast_fusion.9 = f32[27,130,4,130]{3,0,2,1:T(8,128)} fusion(bf16[4,16,130,4,130]{4,1,3,2,0:T(8,128)(2,1)} %get-tuple-element.604, s32[]{:T(128)S(6)} %select_n.31, bf16[16,81]{1,0:T(8,128)(2,1)S(1)} %get-tuple-element.605), kind=kOutput, calls=%fused_computation.59.clone.1.clone | convolution fusion | flops 58406400 | bytes 11563236 | tf_op jit(solution)/shard_map/while/body/eval_jaxpr/dot_general | solution.py:81
  558.8 10.4 %convolution_bitcast_fusion.11 = f32[27,130,4,130]{3,0,2,1:T(8,128)} fusion(bf16[4,16,130,4,130]{4,1,3,2,0:T(8,128)(2,1)} %get-tuple-element.604, s32[]{:T(128)S(6)} %select_n.33, bf16[16,81]{1,0:T(8,128)(2,1)S(1)} %get-tuple-element.605), kind=kOutput, calls=%fused_computation.61.clone.1.clone | convolution fusion | flops 58406400 | bytes 11563236 | tf_op jit(solution)/shard_map/while/body/eval_jaxpr/dot_general | solution.py:81
  569.2 47.3 %slice_add_fusion.82 = f32[1,128,2,128]{3,0,2,1:T(1,128)S(1)} fusion(f32[27,130,4,130]{3,0,2,1:T(8,128)} %convolution_bitcast_fusion.9, f32[27,130,4,130]{3,0,2,1:T(8,128)} %convolution_bitcast_fusion.10, f32[27,130,4,130]{3,0,2,1:T(8,128)} %convolution_bitcast_fusion.11), kind=kLoop, calls=%fused_computation.68.clone.1.clone | loop fusion | flops 2621440 | bytes 10747904 | tf_op jit(solution)/shard_map/while/body/eval_jaxpr/add | solution.py:91
  618.5 10.6 %convolution_bitcast_fusion.10 = f32[27,130,4,130]{3,0,2,1:T(8,128)} fusion(bf16[4,16,130,4,130]{4,1,3,2,0:T(8,128)(2,1)} %get-tuple-element.604, s32[]{:T(128)S(6)} %select_n.32, bf16[16,81]{1,0:T(8,128)(2,1)S(1)} %get-tuple-element.605), kind=kOutput, calls=%fused_computation.60.clone.1.clone | convolution fusion | flops 58406400 | bytes 11563236 | tf_op jit(solution)/shard_map/while/body/eval_jaxpr/dot_general | solution.py:81
  630.4 10.5 %convolution_bitcast_fusion.9 = f32[27,130,4,130]{3,0,2,1:T(8,128)} fusion(bf16[4,16,130,4,130]{4,1,3,2,0:T(8,128)(2,1)} %get-tuple-element.604, s32[]{:T(128)S(6)} %select_n.31, bf16[16,81]{1,0:T(8,128)(2,1)S(1)} %get-tuple-element.605), kind=kOutput, calls=%fused_computation.59.clone.1.clone | convolution fusion | flops 58406400 | bytes 11563236 | tf_op jit(solution)/shard_map/while/body/eval_jaxpr/dot_general | solution.py:81
  642.8 10.4 %convolution_bitcast_fusion.11 = f32[27,130,4,130]{3,0,2,1:T(8,128)} fusion(bf16[4,16,130,4,130]{4,1,3,2,0:T(8,128)(2,1)} %get-tuple-element.604, s32[]{:T(128)S(6)} %select_n.33, bf16[16,81]{1,0:T(8,128)(2,1)S(1)} %get-tuple-element.605), kind=kOutput, calls=%fused_computation.61.clone.1.clone | convolution fusion | flops 58406400 | bytes 11563236 | tf_op jit(solution)/shard_map/while/body/eval_jaxpr/dot_general | solution.py:81
  653.2 47.3 %slice_add_fusion.82 = f32[1,128,2,128]{3,0,2,1:T(1,128)S(1)} fusion(f32[27,130,4,130]{3,0,2,1:T(8,128)} %convolution_bitcast_fusion.9, f32[27,130,4,130]{3,0,2,1:T(8,128)} %convolution_bitcast_fusion.10, f32[27,130,4,130]{3,0,2,1:T(8,128)} %convolution_bitcast_fusion.11), kind=kLoop, calls=%fused_computation.68.clone.1.clone | loop fusion | flops 2621440 | bytes 10747904 | tf_op jit(solution)/shard_map/while/body/eval_jaxpr/add | solution.py:91
  (200 shorter events, 133.6 us)
Async XLA Ops:
  0.0 100.3 %copy-start.3 = (bf16[16,81]{1,0:T(8,128)(2,1)S(1)}, bf16[16,81]{1,0:T(8,128)(2,1)}, u32[]{:S(2)}) copy-start(bf16[16,81]{1,0:T(8,128)(2,1)} %param.12) | copy-start | bytes 7780
  0.0 100.3 %copy-start.4 = (f32[16]{0:T(128)S(1)}, f32[16]{0:T(128)}, u32[]{:S(2)}) copy-start(f32[16]{0:T(128)} %param.13) | copy-start | bytes 196
  67.9 12.0 %collective-permute-start = (bf16[1,128,2,128]{3,1,2,0:T(8,128)(2,1)S(1)}, bf16[1,128,2,128]{3,1,2,0:T(8,128)(2,1)S(1)}, u32[]{:S(2)}, u32[]{:S(2)}) collective-permute-start(bf16[1,128,2,128]{3,1,2,0:T(8,128)(2,1)S(1)} %get-tuple-element.225), channel_id=1, source_target_pairs={{0,16},{16,32},{32,48},{48,64},{64,80},{80,96},{96,112},{112,128},... | collective-permute-start | bytes 196616 | tf_op jit(solution)/shard_map/ppermute | solution.py:15
  70.2 11.6 %collective-permute-start.1 = (bf16[1,128,2,128]{3,1,2,0:T(8,128)(2,1)S(1)}, bf16[1,128,2,128]{3,1,2,0:T(8,128)(2,1)S(1)}, u32[]{:S(2)}, u32[]{:S(2)}) collective-permute-start(bf16[1,128,2,128]{3,1,2,0:T(8,128)(2,1)S(1)} %get-tuple-element.226), channel_id=1, source_target_pairs={{16,0},{32,16},{48,32},{64,48},{80,64},{96,80},{112,96},{128,112},... | collective-permute-start | bytes 196616 | tf_op jit(solution)/shard_map/ppermute | solution.py:17
  81.8 8.2 %collective-permute-start.2 = (bf16[4,128,1,128]{3,1,2,0:T(8,128)(2,1)S(1)}, bf16[4,128,1,128]{3,1,2,0:T(8,128)(2,1)S(1)}, u32[]{:S(2)}, u32[]{:S(2)}) collective-permute-start(bf16[4,128,1,128]{3,1,2,0:T(8,128)(2,1)S(1)} %get-tuple-element.223), channel_id=1, source_target_pairs={{0,1},{1,2},{2,3},{3,4},{4,5},{5,6},{6,7},{7,8},{8,9},{9,10},{10,1... | collective-permute-start | bytes 393224 | tf_op jit(solution)/shard_map/ppermute | solution.py:15
  87.5 11.0 %collective-permute-start.3 = (bf16[4,128,1,128]{3,1,2,0:T(8,128)(2,1)S(1)}, bf16[4,128,1,128]{3,1,2,0:T(8,128)(2,1)}, u32[]{:S(2)}, u32[]{:S(2)}) collective-permute-start(bf16[4,128,1,128]{3,1,2,0:T(8,128)(2,1)S(1)} %get-tuple-element.224), channel_id=1, source_target_pairs={{1,0},{2,1},{3,2},{4,3},{5,4},{6,5},{7,6},{8,7},{9,8},{10,9},{11,1... | collective-permute-start | bytes 393224 | tf_op jit(solution)/shard_map/ppermute | solution.py:17
  90.0 0.7 copy-start.2
  326.0 38.3 %collective-permute-start.4 = (bf16[1,16,128,2,128]{4,1,3,2,0:T(8,128)(2,1)S(1)}, bf16[1,16,128,2,128]{4,1,3,2,0:T(8,128)(2,1)S(1)}, u32[]{:S(2)}, u32[]{:S(2)}) collective-permute-start(bf16[1,16,128,2,128]{4,1,3,2,0:T(8,128)(2,1)S(1)} %get-tuple-element.221), channel_id=1, source_target_pairs={{0,16},{16,32},{32,48},{48,64},{64,80},{80,96},{96,112},{112,128},... | collective-permute-start | bytes 3145736 | tf_op jit(solution)/shard_map/ppermute | solution.py:15
  329.8 34.5 %collective-permute-start.5 = (bf16[1,16,128,2,128]{4,1,3,2,0:T(8,128)(2,1)S(1)}, bf16[1,16,128,2,128]{4,1,3,2,0:T(8,128)(2,1)S(1)}, u32[]{:S(2)}, u32[]{:S(2)}) collective-permute-start(bf16[1,16,128,2,128]{4,1,3,2,0:T(8,128)(2,1)S(1)} %get-tuple-element.222), channel_id=1, source_target_pairs={{16,0},{32,16},{48,32},{64,48},{80,64},{96,80},{112,96},{128,112},... | collective-permute-start | bytes 3145736 | tf_op jit(solution)/shard_map/ppermute | solution.py:17
  364.3 1.0 copy-start
  368.5 55.0 %collective-permute-start.6 = (bf16[4,16,128,1,128]{4,1,3,2,0:T(8,128)(2,1)}, bf16[4,16,128,1,128]{4,1,3,2,0:T(8,128)(2,1)}, u32[]{:S(2)}, u32[]{:S(2)}) collective-permute-start(bf16[4,16,128,1,128]{4,1,3,2,0:T(8,128)(2,1)} %get-tuple-element.219), channel_id=1, source_target_pairs={{0,1},{1,2},{2,3},{3,4},{4,5},{5,6},{6,7},{7,8},{8,9},{9,10},{10,1... | collective-permute-start | bytes 6291464 | tf_op jit(solution)/shard_map/ppermute | solution.py:15
  373.5 136.6 %collective-permute-start.7 = (bf16[4,16,128,1,128]{4,1,3,2,0:T(8,128)(2,1)}, bf16[4,16,128,1,128]{4,1,3,2,0:T(8,128)(2,1)}, u32[]{:S(2)}, u32[]{:S(2)}) collective-permute-start(bf16[4,16,128,1,128]{4,1,3,2,0:T(8,128)(2,1)} %get-tuple-element.220), channel_id=1, source_target_pairs={{1,0},{2,1},{3,2},{4,3},{5,4},{6,5},{7,6},{8,7},{9,8},{10,9},{11,1... | collective-permute-start | bytes 6291464 | tf_op jit(solution)/shard_map/ppermute | solution.py:17
  384.0 148.6 %copy-start.1 = (bf16[16,81]{1,0:T(8,128)(2,1)S(1)}, bf16[16,81]{1,0:T(8,128)(2,1)}, u32[]{:S(2)}) copy-start(bf16[16,81]{1,0:T(8,128)(2,1)} %param.14) | copy-start | bytes 7780
where the time goes:
time: 708 us; the launch traced here: 701 us
  local copies, waits for them, and re-layouts  220 us (31%)
  waiting for transfers between devices  165 us (23%)
  other arithmetic  124 us (18%)
  matrix products  70.7 us (10%)
  blocking collectives  64.1 us (9%)
  starting transfers between devices  43.8 us (6%)
  loops' own time  13.4 us (2%)
    while x162, local copies, waits for them, and re-layouts  120 us
    ppermute x4, waiting for transfers between devices, extended(): lax.ppermute(head, axis, [((i + 1) % count, i) for i in range(ends)])  96.3 us
    add x2, other arithmetic, second_one_row(): total + taps[9 * t_j + 3 * t_k + t_l, t_j:t_j + width_j, t_k:t_k + out_k,...  94.6 us
    another operation x2, local copies, waits for them, and re-layouts, first_one_row(): jnp.stack([block[t_i, t_j:t_j + width_j, t_k:t_k + out_k, t_l:t_l + width...  83.1 us
    ppermute x4, waiting for transfers between devices, extended(): lax.ppermute(tail, axis, [(i, (i + 1) % count) for i in range(ends)])  68.9 us
    dot_general x6, matrix products, second_one_row(): lax.dot_general(weight_two[:, 27 * t_i:27 * t_i + 27], plane, (((0,), (0,...  63 us
    all_gather x1, blocking collectives, correlate(): gathered = lax.all_gather(norm_a, 'rb', axis=1, tiled=True)  36.8 us
    all_gather x1, blocking collectives, correlate(): piece = lax.all_gather(norm_b, 'ra', axis=1, tiled=True)  27.3 us
  transfers between devices with their start and end apart: 8, of which 6 were waited for; matrix products, arithmetic and copies ran while one was open for 0% of the time, Pallas kernels for 0%

commit v1 on v0

v1 whole, which is shorter than its diff:
```python
import functools

import jax
import jax.numpy as jnp
import ml_dtypes
import numpy as np
from jax import lax
from jax.experimental import pallas as pl
from jax.experimental.pallas import tpu as pltpu
from jax.sharding import PartitionSpec as P

HID = 16
LANES = 128
COLS = 512
USED = 432


def first_selector():
    table = np.zeros((81, 16, COLS), np.float32)
    for io in range(4):
        for ko in range(4):
            for a in range(3):
                for b in range(3):
                    for c in range(3):
                        for d in range(3):
                            col = ((b * 3 + d) * 6 + ko + c) * 8 + io + a
                            table[27 * a + 9 * b + 3 * c + d, io * 4 + ko, col] = 1
    return table.reshape(81, 16 * COLS).astype(ml_dtypes.bfloat16)


def second_selector():
    taps = np.zeros((9, 72, 81), np.float32)
    places = np.zeros((9, 72, 256), np.float32)
    for a in range(3):
        for c in range(3):
            for b in range(3):
                for d in range(3):
                    for i in range(2):
                        for k in range(2):
                            row = (b * 3 + d) * 8 + i * 2 + k
                            taps[a * 3 + c, row, 27 * a + 9 * b + 3 * c + d] = 1
                            start = ((i + a) * 4 + k + c) * HID
                            places[a * 3 + c, row, start : start + HID] = 1
    return (
        taps.reshape(648, 81).astype(ml_dtypes.bfloat16),
        places.reshape(648, 256).astype(ml_dtypes.bfloat16),
    )


def row_selector():
    table = np.zeros((64, 48), np.float32)
    for jj in range(8):
        for ii in range(6):
            table[jj * 8 + ii, ii * 8 + jj] = 1
    return table.astype(ml_dtypes.bfloat16)


def channel_tiler():
    return np.tile(np.eye(HID, dtype=np.float32), (1, 16)).astype(ml_dtypes.bfloat16)


def normalized(ref):
    values = ref[...].astype(jnp.float32)
    scale = lax.rsqrt(jnp.sum(values * values, axis=-1, keepdims=True) + 1e-06)
    return (values * scale).reshape(16, values.shape[-1]).astype(jnp.bfloat16)


def in_range(index, count):
    return jnp.logical_and(index >= 0, index < count)


class Copies:
    def __init__(self, send_sem, recv_sem):
        self.send_sem, self.recv_sem = send_sem, recv_sem
        self.started = []

    def start(self, src, dst, device):
        n = len(self.started)
        copy = pltpu.make_async_remote_copy(
            src_ref=src,
            dst_ref=dst,
            send_sem=self.send_sem.at[n],
            recv_sem=self.recv_sem.at[n],
            device_id=device,
            device_id_type=pl.DeviceIdType.MESH,
        )
        copy.start()
        self.started.append(copy)
        return copy


N_COPIES = 95


def place(ra, rb):
    x, zh, c = lax.div(ra, 4), lax.rem(lax.div(ra, 2), 2), lax.rem(ra, 2)
    y, zl = lax.div(rb, 4), lax.rem(rb, 4)
    return x, zh, c, y, zl


def greet(ra, rb):
    x, zh, c, y, zl = place(ra, rb)
    step = 2 * c - 1
    outer = lax.rem(ra + step + 16, 16)
    partners = [(outer, rb), (ra - step, rb), ((x * 2 + 1 - zh) * 2 + c, rb)]
    partners += [(ra, y * 4 + lax.rem(zl + t, 4)) for t in (1, 2, 3)]
    partners += [(ra, lax.rem(rb + t, 16)) for t in (4, 12)]
    partners += [(ra, lax.rem(rb + t, 16)) for t in (1, 15)]
    partners += [(lax.rem(ra + t, 16), rb) for t in (4, 12)]
    barrier = pltpu.get_barrier_semaphore()
    for device in partners:
        pl.semaphore_signal(barrier, inc=1, device_id=device, device_id_type=pl.DeviceIdType.MESH)
    return barrier, len(partners)


def gather(ra, rb, a_rows, b_rows, send_sem, recv_sem, meanwhile):
    copies = Copies(send_sem, recv_sem)
    x, zh, c, y, zl = place(ra, rb)
    step = 2 * c - 1
    outer = (lax.rem(ra + step + 16, 16), rb)
    mate = (ra - step, rb)
    far = ((x * 2 + 1 - zh) * 2 + c, rb)
    right_y, left_y = (ra, lax.rem(rb + 4, 16)), (ra, lax.rem(rb + 12, 16))
    right_x, left_x = (lax.rem(ra + 4, 16), rb), (lax.rem(ra + 12, 16), rb)
    next_b, prev_b = (ra, lax.rem(rb + 1, 16)), (ra, lax.rem(rb + 15, 16))
    ro = 2 * c
    mate_slot = 2 - 2 * (1 - c)

    def mate_a(index, count=1):
        part = pl.ds(index, count)
        return copies.start(a_rows.at[1, part], a_rows.at[mate_slot, part], mate)

    def mate_b(q, index, count=1):
        part = pl.ds(index, count)
        return copies.start(b_rows.at[q, c, part], b_rows.at[q, c, part], mate)

    def chunk_a(slot, index):
        return a_rows.at[slot, index]

    def chunk_b(q, index):
        return b_rows.at[q, c, index]

    def to_y(slot, index):
        return [
            copies.start(chunk_a(slot, index), chunk_a(slot, index), d) for d in (right_y, left_y)
        ]

    def to_x(q, index):
        return [copies.start(chunk_b(q, index), chunk_b(q, index), d) for d in (right_x, left_x)]

    here, there = x * 2 + zh, x * 2 + 1 - zh
    columns = [y * 4 + lax.rem(zl + 4 - t, 4) for t in range(4)]

    def to_z(slot):
        return [
            copies.start(chunk_a(slot, rb), chunk_a(slot, rb), (ra, y * 4 + lax.rem(zl + t, 4)))
            for t in (1, 2, 3)
        ]

    def to_rb(index):
        return [
            copies.start(chunk_b(1, index), chunk_b(0, index), next_b),
            copies.start(chunk_b(1, index), chunk_b(2, index), prev_b),
        ]

    mates = []
    b_far = copies.start(chunk_b(1, here), chunk_b(1, here), far)
    a_outer = copies.start(chunk_a(1, rb), chunk_a(2 - ro, rb), outer)
    z_own = to_z(1)
    rb_own = to_rb(here)
    y_own = [to_y(1, rb)]
    x_own = [to_x(1, here)]
    mates.append(mate_a(rb))
    mates.append(mate_b(1, here))

    meanwhile()

    b_far.wait_recv()
    rb_far = to_rb(there)
    x_far = [to_x(1, there)]
    mates.append(mate_b(1, there))

    a_outer.wait_recv()
    z_outer = to_z(ro)
    y_outer = [to_y(ro, rb)]

    for q, copy in ((0, rb_own[0]), (2, rb_own[1])):
        copy.wait_recv()
        x_own.append(to_x(q, here))
        mates.append(mate_b(q, here))

    for t in (1, 2, 3):
        z_own[t - 1].wait_recv()
        y_own.append(to_y(1, columns[t]))
        mates.append(mate_a(columns[t]))

    for q, copy in ((0, rb_far[0]), (2, rb_far[1])):
        copy.wait_recv()
        x_far.append(to_x(q, there))
        mates.append(mate_b(q, there))

    for t in (1, 2, 3):
        z_outer[t - 1].wait_recv()
        y_outer.append(to_y(ro, columns[t]))

    on_left = lax.rem(x + 3, 4) * 2
    on_right = lax.rem(x + 1, 4) * 2
    x_on = []
    own_right = zh == 0
    for q in range(3):
        pairs = (x_own[(1, 0, 2)[q]], x_far[(1, 0, 2)[q]])
        for pair in pairs:
            for copy in pair:
                copy.wait_recv()
        x_on.append(copies.start(chunk_b(q, on_left), chunk_b(q, on_left), right_x))
        x_on.append(copies.start(chunk_b(q, on_right + 1), chunk_b(q, on_right + 1), left_x))
        mates.append(mate_b(q, on_left, 2))
        mates.append(mate_b(q, on_right, 2))
    del own_right

    left_col = [lax.rem(y + 3, 4) * 4 + lax.rem(zl + 4 - t, 4) for t in range(4)]
    right_col = [lax.rem(y + 1, 4) * 4 + lax.rem(zl + 4 - t, 4) for t in range(4)]
    y_on = []
    for t in range(4):
        y_own[t][0].wait_recv()
        y_on.append(copies.start(chunk_a(1, left_col[t]), chunk_a(1, left_col[t]), right_y))
        y_own[t][1].wait_recv()
    for side in (3, 1):
        mates.append(mate_a(lax.rem(y + side, 4) * 4, 4))
    for t in range(4):
        y_outer[t][1].wait_recv()
        y_on.append(copies.start(chunk_a(ro, right_col[t]), chunk_a(ro, right_col[t]), left_y))
        y_outer[t][0].wait_recv()
    across = lax.rem(x + 2, 4) * 2
    for n, copy in enumerate(x_on):
        copy.wait_recv()
        if n % 2 == 1:
            mates.append(mate_b(n // 2, across, 2))
    for copy in y_on[:4]:
        copy.wait_recv()
    mates.append(mate_a(lax.rem(y + 2, 4) * 4, 4))
    for copy in y_on[4:]:
        copy.wait_recv()
    for copy in mates:
        copy.wait_recv()
    assert len(copies.started) <= N_COPIES, len(copies.started)
    return copies


def weights(ra, rb, w1_ref, bias1_ref, w2_ref, sel1, taps2, places2, tiler, big1, bias_big, big2):
    f32 = jnp.float32
    bias = bias1_ref[...]
    w1 = w1_ref[...]
    for io in range(4):
        for ko in range(4):
            n = io * 4 + ko
            inside = jnp.logical_and(in_range(2 * ra - 1 + io, 32), in_range(2 * rb - 1 + ko, 32))
            inside = inside.astype(f32)
            block = jnp.dot(w1, sel1[:, n * COLS : (n + 1) * COLS], preferred_element_type=f32)
            big1[n * HID : (n + 1) * HID, :] = (block * inside).astype(jnp.bfloat16)
            bias_big[n * HID : (n + 1) * HID, :] = bias * inside
    spread = lax.dot_general(
        w2_ref[...], tiler[...], (((0,), (0,)), ((), ())), preferred_element_type=f32
    ).astype(jnp.bfloat16)
    terms = jnp.dot(taps2[...], spread, preferred_element_type=f32) * places2[...].astype(f32)
    total = terms[0:72]
    for n in range(1, 9):
        total = total + terms[72 * n : 72 * n + 72]
    big2[...] = total.astype(jnp.bfloat16)


def shifted(values, by):
    lane = lax.broadcasted_iota(jnp.int32, values.shape, values.ndim - 1)
    moved = pltpu.roll(values, (-by) % LANES, values.ndim - 1)
    return jnp.where(lane == (0 if by < 0 else LANES - 1), jnp.zeros_like(moved), moved)


def arrange(ra, rb, a_rows, b_rows, rows, a_perm, b_perm):
    f32 = jnp.float32
    row = lax.broadcasted_iota(jnp.int32, (64, 48), 0)
    inside = in_range(2 * ra - 2 + lax.rem(row, 8), 32)
    select = jnp.where(inside, rows[...].astype(f32), 0.0).astype(jnp.bfloat16)

    def one_a(n, _):
        part = jnp.concatenate([a_rows[r, n] for r in range(3)], axis=0)
        a_perm[pl.ds(pl.multiple_of(n * 64, 64), 64), :] = jnp.dot(
            select, part, preferred_element_type=f32
        ).astype(jnp.bfloat16)
        return 0

    lax.fori_loop(0, 16, one_a, 0)
    for q in range(3):
        valid = in_range(rb - 1 + q, 16)
        for n in range(8):
            both = [b_rows[q, c, n].astype(f32) for c in range(2)]
            for k in range(2):
                rows16 = jnp.concatenate([v[8 * k : 8 * k + 8] for v in both], axis=0)
                b_perm[2 * q + k, 16 * n : 16 * n + 16, :] = jnp.where(
                    valid, rows16, 0.0
                ).astype(jnp.bfloat16)


J_STEP = 32


def correlate(a_perm, b_perm, patches):
    f32 = jnp.float32
    zero = jnp.zeros((9, 16, LANES), jnp.bfloat16)
    patches[0] = zero
    patches[129] = zero

    def one(n, _):
        part = a_perm[pl.ds(pl.multiple_of(n * J_STEP * 8, J_STEP * 8), J_STEP * 8), :]
        for pair in range(3):
            both = []
            for k in range(2):
                corr = lax.dot_general(
                    part, b_perm[2 * pair + k], (((1,), (1,)), ((), ())), preferred_element_type=f32
                )
                both.append(corr.reshape(J_STEP, 8, LANES))
            tile = jnp.concatenate(both, axis=1)
            for s in range(3):
                moved = tile if s == 1 else shifted(tile, s - 1)
                patches[pl.ds(1 + n * J_STEP, J_STEP), s * 3 + pair] = moved.astype(jnp.bfloat16)
        return 0

    lax.fori_loop(0, 128 // J_STEP, one, 0)


UNROLL = 2


def layers(patches, big1, bias_big, big2, taps):
    f32 = jnp.float32
    zero = jnp.zeros((72, LANES), f32)
    taps[0] = zero
    taps[129] = zero

    def one(n, _):
        for u in range(UNROLL):
            j = (n * UNROLL + u) * 2
            left = patches[pl.ds(j, 3)].reshape(USED, LANES)
            right = patches[pl.ds(j + 1, 3)].reshape(USED, LANES)
            before = jnp.dot(
                big1[:, :USED], jnp.concatenate([left, right], axis=1), preferred_element_type=f32
            )
            bias = bias_big[...]
            hidden = jnp.maximum(before + jnp.concatenate([bias, bias], axis=1), 0.0)
            out = jnp.dot(big2[...], hidden.astype(jnp.bfloat16), preferred_element_type=f32)
            taps[j + 1] = out[:, :LANES]
            taps[j + 2] = out[:, LANES:]
        return 0

    lax.fori_loop(0, 64 // UNROLL, one, 0)


def finish(taps, bias2, out_ref):
    step = 16

    def one(n, _):
        start = n * step
        sums = []
        for d in range(3):
            total = None
            for b in range(3):
                row = (b * 3 + d) * 8
                part = taps[pl.ds(start + b, step), row : row + 8]
                total = part if total is None else total + part
            sums.append(total)
        value = sums[1] + shifted(sums[0], -1) + shifted(sums[2], 1)
        value = jnp.maximum(value + bias2, 0.0)
        out_ref[0, pl.ds(start, step)] = value[:, 0:2]
        out_ref[1, pl.ds(start, step)] = value[:, 2:4]
        return 0

    lax.fori_loop(0, 128 // step, one, 0)


def kernel(
    a_ref, b_ref, w1_ref, bias1_ref, w2_ref, bias2_ref, sel1, taps2, places2, tiler, rows,
    out_ref,
    a_rows, b_rows, a_perm, b_perm, patches, taps, big1, bias_big, big2, send_sem, recv_sem,
):
    ra, rb = lax.axis_index("ra"), lax.axis_index("rb")
    x, zh, c, _, _ = place(ra, rb)
    barrier, count = greet(ra, rb)
    a_rows[1, rb] = normalized(a_ref)
    b_rows[1, c, x * 2 + zh] = normalized(b_ref)
    pl.semaphore_wait(barrier, count)
    copies = gather(
        ra, rb, a_rows, b_rows, send_sem, recv_sem,
        functools.partial(
            weights, ra, rb, w1_ref, bias1_ref, w2_ref, sel1, taps2, places2, tiler,
            big1, bias_big, big2,
        ),
    )
    arrange(ra, rb, a_rows, b_rows, rows, a_perm, b_perm)
    correlate(a_perm, b_perm, patches)
    layers(patches, big1, bias_big, big2, taps)
    finish(taps, bias2_ref[0], out_ref)
    for copy in copies.started:
        copy.wait_send()


SEL1 = first_selector()
TAPS2, PLACES2 = second_selector()
ROWS = row_selector()
TILER = channel_tiler()


def compute_scratch(channels):
    bf16, f32 = jnp.bfloat16, jnp.float32
    return [
        pltpu.VMEM((3, 16, 16, channels), bf16),
        pltpu.VMEM((3, 2, 8, 16, channels), bf16),
        pltpu.VMEM((1024, channels), bf16),
        pltpu.VMEM((6, LANES, channels), bf16),
        pltpu.VMEM((130, 9, 16, LANES), bf16),
        pltpu.VMEM((130, 72, LANES), f32),
        pltpu.VMEM((256, COLS), bf16),
        pltpu.VMEM((256, LANES), f32),
        pltpu.VMEM((72, 256), bf16),
    ]


def per_device(features_a, features_b, weight_one, bias_one, weight_two, bias_two):
    channels = features_a.shape[-1]
    vmem = pl.BlockSpec(memory_space=pltpu.VMEM)
    bias_cols = jnp.broadcast_to(bias_one[:, None], (HID, LANES))
    return pl.pallas_call(
        kernel,
        out_shape=jax.ShapeDtypeStruct((2, LANES, 2, LANES), jnp.float32),
        in_specs=[vmem] * 5 + [pl.BlockSpec(memory_space=pltpu.SMEM)] + [vmem] * 5,
        out_specs=vmem,
        scratch_shapes=compute_scratch(channels)
        + [pltpu.SemaphoreType.DMA((N_COPIES,)), pltpu.SemaphoreType.DMA((N_COPIES,))],
        compiler_params=pltpu.CompilerParams(
            collective_id=0, has_side_effects=True, vmem_limit_bytes=48 * 1024 * 1024
        ),
        name="consensus",
    )(
        features_a, features_b, weight_one, bias_cols, weight_two, bias_two,
        SEL1, TAPS2, PLACES2, TILER, ROWS,
    )


def solution(mesh):
    return jax.shard_map(
        per_device,
        mesh=mesh,
        in_specs=(P("ra", "rb", None), P("rb", "ra", None), P(), P(), P(), P()),
        out_specs=P("ra", None, "rb", None),
        check_vma=False,
    )
```

time: 708 us -> 73.9 us (0.10)
  the two profiles are of different devices: /device:TPU:232 before, /device:TPU:1 now
where the time goes in v1:
time: 73.9 us; the launch traced here: 73.5 us
  Pallas kernels  63.8 us (86%)
  local copies, waits for them, and re-layouts  8.98 us (12%)
    pallas_call x1, Pallas kernels, per_device(): pl.pallas_call(kernel, out_shape=jax.ShapeDtypeStruct((2, LANES, 2, LANES...  63.8 us
    unnamed x19, local copies, waits for them, and re-layouts  8.26 us

profile of v1, /device:TPU:1, one launch (start us, length us, event | category | flops | bytes accessed | tf_op | source)
XLA Modules:
  0.0 73.5 jit_solution(15353033124280649406)
XLA Ops:
  0.7 0.7 broadcast_in_dim.2.bias1_ref
  1.4 0.0 copy-start
  1.4 1.4 %copy-done = bf16[81,8192]{1,0:T(8,128)(2,1)S(1)} copy-done((bf16[81,8192]{1,0:T(8,128)(2,1)S(1)}, bf16[81,8192]{1,0:T(8,128)(2,1)}, u32[]{:S(2)}) %copy-start) | copy-done | bytes 1327128
  2.7 0.0 copy-start.1
  2.7 1.0 %copy-done.1 = bf16[648,256]{1,0:T(8,128)(2,1)S(1)} copy-done((bf16[648,256]{1,0:T(8,128)(2,1)S(1)}, bf16[648,256]{1,0:T(8,128)(2,1)}, u32[]{:S(2)}) %copy-start.1) | copy-done | bytes 331800
  3.7 0.0 copy-start.2
  3.7 0.9 %copy-done.2 = bf16[648,81]{1,0:T(8,128)(2,1)S(1)} copy-done((bf16[648,81]{1,0:T(8,128)(2,1)S(1)}, bf16[648,81]{1,0:T(8,128)(2,1)}, u32[]{:S(2)}) %copy-start.2) | copy-done | bytes 105000
  4.6 0.0 copy-start.3
  4.6 0.8 %copy-done.3 = bf16[2,8,1024]{2,1,0:T(8,128)(2,1)S(1)} copy-done((bf16[2,8,1024]{2,1,0:T(8,128)(2,1)S(1)}, bf16[2,8,1024]{2,1,0:T(8,128)(2,1)}, u32[]{:S(2)}) %copy-start.3) | copy-done | bytes 32792
  5.4 0.0 copy-start.4
  5.4 0.8 %copy-done.4 = bf16[2,8,1024]{2,1,0:T(8,128)(2,1)S(1)} copy-done((bf16[2,8,1024]{2,1,0:T(8,128)(2,1)S(1)}, bf16[2,8,1024]{2,1,0:T(8,128)(2,1)}, u32[]{:S(2)}) %copy-start.4) | copy-done | bytes 32792
  6.2 0.0 copy-start.5
  6.2 0.7 copy-done.5
  6.9 0.0 copy-start.6
  6.9 0.7 copy-done.6
  7.6 0.0 copy-start.7
  7.6 0.7 copy-done.7
  8.3 0.0 copy-start.8
  8.3 0.7 copy-done.8
  8.9 63.8 %consensus.1 = f32[2,128,2,128]{3,2,1,0:T(2,128)S(1)} custom-call(bf16[2,8,1024]{2,1,0:T(8,128)(2,1)S(1)} %copy-done.3, bf16[2,8,1024]{2,1,0:T(8,128)(2,1)S(1)} %copy-done.4, bf16[16,81]{1,0:T(8,128)(2,1)S(1)} %copy-done.7, f32[16,128]{1,0:T(8,128)S(1)} %broadcast_in_dim.2.bias1_ref, bf16[16,81]{1,0:T(8,128)(2,1)S(1)} %copy-done.8, f32[1]{0:T(128)S(6)} %copy.13.bias2_ref, ...), custom_call_target="tpu_custom_call" | custom-call | tf_op jit(solution)/shard_map/consensus/pallas_call | solution.py:430
  72.7 0.7 copy.14
Async XLA Ops:
  1.4 1.4 %copy-start = (bf16[81,8192]{1,0:T(8,128)(2,1)S(1)}, bf16[81,8192]{1,0:T(8,128)(2,1)}, u32[]{:S(2)}) copy-start(bf16[81,8192]{1,0:T(8,128)(2,1)} %constant.10.clone.sel1) | copy-start | bytes 3981316
  2.7 1.0 %copy-start.1 = (bf16[648,256]{1,0:T(8,128)(2,1)S(1)}, bf16[648,256]{1,0:T(8,128)(2,1)}, u32[]{:S(2)}) copy-start(bf16[648,256]{1,0:T(8,128)(2,1)} %constant.12.clone.places2) | copy-start | bytes 995332
  3.7 0.9 %copy-start.2 = (bf16[648,81]{1,0:T(8,128)(2,1)S(1)}, bf16[648,81]{1,0:T(8,128)(2,1)}, u32[]{:S(2)}) copy-start(bf16[648,81]{1,0:T(8,128)(2,1)} %constant.11.clone.taps2) | copy-start | bytes 314932
  4.6 0.8 %copy-start.3 = (bf16[2,8,1024]{2,1,0:T(8,128)(2,1)S(1)}, bf16[2,8,1024]{2,1,0:T(8,128)(2,1)}, u32[]{:S(2)}) copy-start(bf16[2,8,1024]{2,1,0:T(8,128)(2,1)} %a_ref.1) | copy-start | bytes 98308
  5.4 0.8 %copy-start.4 = (bf16[2,8,1024]{2,1,0:T(8,128)(2,1)S(1)}, bf16[2,8,1024]{2,1,0:T(8,128)(2,1)}, u32[]{:S(2)}) copy-start(bf16[2,8,1024]{2,1,0:T(8,128)(2,1)} %b_ref.1) | copy-start | bytes 98308
  6.2 0.7 copy-start.5
  6.9 0.7 copy-start.6
  7.6 0.7 copy-start.7
  8.3 0.7 copy-start.8

commit v2 on v0

v2 whole, which is shorter than its diff:
```python
import jax
import jax.numpy as jnp
from jax import lax
from jax.experimental import pallas as pl
from jax.experimental.pallas import tpu as pltpu
from jax.sharding import PartitionSpec as P

HID = 16
LANES = 128
COLS = 512
USED = 432
CELLS = 24
HALF = 64
CHUNKS = 9


def steps(values, size, count):
    total = jnp.zeros_like(values)
    for n in range(1, count):
        total = total + (values >= n * size).astype(jnp.int32)
    return total


def iota(shape, axis):
    return lax.broadcasted_iota(jnp.int32, shape, axis)


def as_bf16(mask):
    return jnp.where(mask, 1.0, 0.0).astype(jnp.bfloat16)


def normalized(ref):
    values = ref[...].astype(jnp.float32)
    scale = lax.rsqrt(jnp.sum(values * values, axis=-1, keepdims=True) + 1e-06)
    return (values * scale).reshape(16, values.shape[-1]).astype(jnp.bfloat16)


def in_range(index, count):
    return jnp.logical_and(index >= 0, index < count)


class Copies:
    def __init__(self, send_sem, recv_sem):
        self.send_sem, self.recv_sem = send_sem, recv_sem
        self.started = []

    def start(self, src, dst, device, arrives=None, later=False):
        n = len(self.started)
        copy = pltpu.make_async_remote_copy(
            src_ref=src,
            dst_ref=dst,
            send_sem=self.send_sem.at[n],
            recv_sem=self.recv_sem.at[n if arrives is None else arrives],
            device_id=device,
            device_id_type=pl.DeviceIdType.MESH,
        )
        if later:
            return copy
        copy.start()
        self.started.append((copy, None))
        return copy

    def start_when(self, copy, when):
        pl.when(when)(copy.start)
        self.started.append((copy, when))

    def wait_send(self):
        for copy, when in self.started:
            if when is None:
                copy.wait_send()
            else:
                pl.when(when)(copy.wait_send)


N_COPIES = 100
CHAIN = N_COPIES


class Place:
    def __init__(self, ra, rb):
        self.ra, self.rb = ra, rb
        self.x, self.zh, self.c = lax.div(ra, 4), lax.rem(lax.div(ra, 2), 2), lax.rem(ra, 2)
        self.y, self.zl = lax.div(rb, 4), lax.rem(rb, 4)
        self.chip = lax.div(ra, 2)
        flipped = (self.x * 2 + 1 - self.zh) * 2 + self.c
        self.mate = (ra + 1 - 2 * self.c, rb)
        self.far = (flipped, rb)
        self.line = [(ra, self.y * 4 + lax.rem(self.zl + t, 4)) for t in (1, 2, 3)]
        self.right_y, self.left_y = (ra, lax.rem(rb + 4, 16)), (ra, lax.rem(rb + 12, 16))
        self.right_x, self.left_x = (lax.rem(ra + 4, 16), rb), (lax.rem(ra + 12, 16), rb)
        self.next_b = (jnp.where(self.zl == 3, flipped, ra), lax.rem(rb + 1, 16))
        self.prev_b = (jnp.where(self.zl == 0, flipped, ra), lax.rem(rb + 15, 16))
        self.outer = lax.rem(ra + 2 * self.c + 15, 16)


def greet(p):
    barrier = pltpu.get_barrier_semaphore()

    def signal(device):
        pl.semaphore_signal(barrier, inc=1, device_id=device, device_id_type=pl.DeviceIdType.MESH)

    partners = [p.mate, p.far, p.right_y, p.left_y, p.right_x, p.left_x, p.next_b, p.prev_b]
    for device in partners + p.line:
        signal(device)

    @pl.when(p.zl == 0)
    def _():
        signal((p.outer, p.y * 4 + 2))
        signal((p.outer, p.y * 4 + 3))

    @pl.when(p.zl == 3)
    def _():
        signal((p.outer, p.y * 4))
        signal((p.outer, p.y * 4 + 1))

    return barrier, len(partners) + len(p.line) + 1


def gather(p, a_rows, b_rows, send_sem, recv_sem, meanwhile, have_b):
    copies = Copies(send_sem, recv_sem)
    x, zh, c, y, zl, rb = p.x, p.zh, p.c, p.y, p.zl, p.rb
    so, oo = 1 + c, 3 * c

    def mate_a(slot, index, count=1):
        part = a_rows.at[slot, pl.ds(index, count)]
        return copies.start(part, part, p.mate)

    def mate_b(q, index, count=1):
        part = b_rows.at[q, c, pl.ds(index, count)]
        return copies.start(part, part, p.mate)

    def chunk_a(slot, index):
        return a_rows.at[slot, index]

    def chunk_b(q, index):
        return b_rows.at[q, c, index]

    def to_y(slot, index):
        mates_a.append(mate_a(slot, index))
        return [
            copies.start(chunk_a(slot, index), chunk_a(slot, index), d)
            for d in (p.right_y, p.left_y)
        ]

    def to_x(q, index):
        mates_b.append(mate_b(q, index))
        return [
            copies.start(chunk_b(q, index), chunk_b(q, index), d) for d in (p.right_x, p.left_x)
        ]

    def to_rb(index):
        return [
            copies.start(chunk_b(1, index), chunk_b(0, index), p.next_b),
            copies.start(chunk_b(1, index), chunk_b(2, index), p.prev_b),
        ]

    here, there = x * 2 + zh, x * 2 + 1 - zh
    mates_a, mates_b = [], []

    end = (p.outer, y * 4 + jnp.where(zl >= 2, 0, 3))
    copies.start(chunk_a(so, rb), chunk_a(3 - oo, rb), end, arrives=CHAIN + zl)
    b_far = copies.start(chunk_b(1, here), chunk_b(1, here), p.far)
    z_own = [copies.start(chunk_a(so, rb), chunk_a(so, rb), d) for d in p.line]
    rb_own = to_rb(here)
    y_own = [to_y(so, rb)]
    x_own = [to_x(1, here)]

    meanwhile()

    near = zl < 2
    y_outer = []

    def chain(source):
        column = y * 4 + source
        onward = jnp.where(source >= 2, zl + 1, zl - 1)
        chunk = chunk_a(oo, column)
        neighbour = (p.ra, y * 4 + lax.rem(onward + 4, 4))
        copy = copies.start(chunk, chunk, neighbour, arrives=CHAIN + source, later=True)
        copy.wait_recv()
        copies.start_when(copy, in_range(onward, 4))
        y_outer.append(to_y(oo, column))

    columns = [y * 4 + lax.rem(zl + 4 - t, 4) for t in range(4)]

    def line(t):
        z_own[t - 1].wait_recv()
        y_own.append(to_y(so, columns[t]))

    chain_order = [jnp.where(near, 3, 0), jnp.where(near, 2, 1), jnp.where(near, 0, 3), jnp.where(near, 1, 2)]
    from_prev = [jnp.where(zl == 0, there, here), jnp.where(zl == 0, here, there)]
    from_next = [jnp.where(zl == 3, there, here), jnp.where(zl == 3, here, there)]

    chain(chain_order[0])
    line(1)
    chain(chain_order[1])
    line(3)
    for q, copy, index in ((0, rb_own[0], from_prev[0]), (2, rb_own[1], from_next[0])):
        copy.wait_recv()
        x_own.append(to_x(q, index))
    line(2)
    b_far.wait_recv()
    rb_far = to_rb(there)
    x_far = [to_x(1, there)]

    left_col = [lax.rem(y + 3, 4) * 4 + lax.rem(zl + 4 - t, 4) for t in range(4)]
    order = (0, 1, 3, 2)
    y_on = []

    def own_on(m):
        y_own[m][0].wait_recv()
        chunk = chunk_a(so, left_col[order[m]])
        y_on.append(copies.start(chunk, chunk, p.right_y))

    own_on(0)
    chain(chain_order[2])
    chain(chain_order[3])
    own_on(1)
    for q, copy, index in ((0, rb_far[0], from_prev[1]), (2, rb_far[1], from_next[1])):
        copy.wait_recv()
        x_far.append(to_x(q, index))
    own_on(2)
    own_on(3)

    on_left, on_right = lax.rem(x + 3, 4) * 2, lax.rem(x + 1, 4) * 2
    x_on = []

    def b_on(m):
        q = (1, 0, 2)[m]
        for pair in (x_own[m], x_far[m]):
            for copy in pair:
                copy.wait_recv()
        for index, device in ((on_left, p.right_x), (on_right + 1, p.left_x)):
            x_on.append(copies.start(chunk_b(q, index), chunk_b(q, index), device))
        mates_b.append(mate_b(q, on_left, 2))
        mates_b.append(mate_b(q, on_right, 2))

    outer_on = []

    def a_on(m):
        y_outer[m][1].wait_recv()
        chunk = chunk_a(oo, lax.rem(y + 1, 4) * 4 + chain_order[m])
        outer_on.append(copies.start(chunk, chunk, p.left_y))

    b_on(0)
    a_on(0)
    a_on(1)
    b_on(1)
    b_on(2)
    a_on(2)
    a_on(3)
    for copy in y_own:
        copy[1].wait_recv()
    for copy in y_outer:
        copy[0].wait_recv()
    for slot in (so, oo):
        for side in (3, 1):
            mates_a.append(mate_a(slot, lax.rem(y + side, 4) * 4, 4))
    across = lax.rem(x + 2, 4) * 2
    for n, copy in enumerate(x_on):
        copy.wait_recv()
        if n % 2 == 1:
            mates_b.append(mate_b((1, 0, 2)[n // 2], across, 2))
    for slot, arrivals in ((so, y_on), (oo, outer_on)):
        for copy in arrivals:
            copy.wait_recv()
        mates_a.append(mate_a(slot, lax.rem(y + 2, 4) * 4, 4))
    for copy in mates_b:
        copy.wait_recv()
    have_b()
    for copy in mates_a:
        copy.wait_recv()
    return copies


def weights(p, w1_ref, bias1_ref, w2_ref, big1, bias_big, big2):
    f32, bf16 = jnp.float32, jnp.bfloat16
    channel = iota((HID, LANES), 0)
    bias = jnp.zeros((HID, LANES), f32)
    for o in range(HID):
        bias = jnp.where(channel == o, bias1_ref[o], bias)
    w1 = w1_ref[...]
    tap = iota((81, COLS), 0)
    col = iota((1, COLS), 1)
    group = steps(col, 48, 11)
    tap_j = steps(group, 3, 4)
    shift = group - 3 * tap_j
    rest = col - 48 * group
    ki = steps(rest, 8, 6)
    ii = rest - 8 * ki
    for io in range(6):
        for ko in range(4):
            n = io * 4 + ko
            inside = jnp.logical_and(in_range(4 * p.chip - 1 + io, 32), in_range(2 * p.rb - 1 + ko, 32))
            inside = inside.astype(f32)
            a, c = ii - io, ki - ko
            fits = jnp.logical_and(jnp.logical_and(a >= 0, a < 3), jnp.logical_and(c >= 0, c < 3))
            wanted = jnp.where(
                jnp.logical_and(fits, col < USED), 27 * a + 9 * tap_j + 3 * c + shift, -1
            )
            block = jnp.dot(w1, as_bf16(tap == wanted), preferred_element_type=f32)
            big1[n * HID : (n + 1) * HID, :] = (block * inside).astype(bf16)
            bias_big[n * HID : (n + 1) * HID, :] = bias * inside
    tile = as_bf16(iota((HID, CELLS * HID), 0) == jnp.bitwise_and(iota((HID, CELLS * HID), 1), HID - 1))
    spread = lax.dot_general(
        w2_ref[...], tile, (((0,), (0,)), ((), ())), preferred_element_type=f32
    ).astype(bf16)
    row = iota((72, 1), 0)
    group = jnp.right_shift(row, 3)
    tap_j = steps(group, 3, 3)
    shift = group - 3 * tap_j
    i = jnp.bitwise_and(jnp.right_shift(row, 1) + 2 * p.c, 3)
    k = jnp.bitwise_and(row, 1)
    cell = jnp.right_shift(iota((72, CELLS * HID), 1), 4)
    tap = iota((72, 81), 1)
    total = jnp.zeros((72, CELLS * HID), f32)
    for a in range(3):
        for c in range(3):
            wanted = 27 * a + 9 * tap_j + 3 * c + shift
            term = jnp.dot(as_bf16(tap == wanted), spread, preferred_element_type=f32)
            total = total + jnp.where(cell == (i + a) * 4 + k + c, term, 0.0)
    big2[...] = total.astype(bf16)


def shifted(values, by):
    lane = lax.broadcasted_iota(jnp.int32, values.shape, values.ndim - 1)
    moved = pltpu.roll(values, (-by) % LANES, values.ndim - 1)
    return jnp.where(lane == (0 if by < 0 else LANES - 1), jnp.zeros_like(moved), moved)


def arrange_a(p, a_rows, a_perm):
    row, col = iota((64, 64), 0), iota((64, 64), 1)
    ii, jj = jnp.bitwise_and(row, 7), jnp.right_shift(row, 3)
    inside = in_range(4 * p.chip - 2 + ii, 32)
    select = as_bf16(jnp.logical_and(inside, col == ii * 8 + jj))
    for n in range(CHUNKS):
        part = jnp.concatenate([a_rows[slot, 7 * p.c + n] for slot in range(4)], axis=0)
        a_perm[n * 64 : (n + 1) * 64, :] = jnp.dot(
            select, part, preferred_element_type=jnp.float32
        ).astype(jnp.bfloat16)


def arrange_b(p, b_rows, b_perm):
    for q in range(3):
        valid = in_range(p.rb - 1 + q, 16)
        for n in range(8):
            both = [b_rows[q, c, n].astype(jnp.float32) for c in range(2)]
            for k in range(2):
                rows16 = jnp.concatenate([v[8 * k : 8 * k + 8] for v in both], axis=0)
                b_perm[2 * q + k, 16 * n : 16 * n + 16, :] = jnp.where(
                    valid, rows16, 0.0
                ).astype(jnp.bfloat16)


J_STEP = 24
EDGE = 8


def correlate(p, a_perm, b_perm, patches):
    f32 = jnp.float32
    patches[pl.ds(CHUNKS * 8 * p.c, EDGE)] = jnp.zeros((EDGE, 9, 16, LANES), jnp.bfloat16)
    base = EDGE * (1 - p.c)
    for n in range(CHUNKS * 8 // J_STEP):
        part = a_perm[n * J_STEP * 8 : (n + 1) * J_STEP * 8, :]
        for pair in range(3):
            both = []
            for k in range(2):
                corr = lax.dot_general(
                    part, b_perm[2 * pair + k], (((1,), (1,)), ((), ())), preferred_element_type=f32
                )
                both.append(corr.reshape(J_STEP, 8, LANES))
            tile = jnp.concatenate(both, axis=1)
            for s in range(3):
                moved = tile if s == 1 else shifted(tile, s - 1)
                patches[pl.ds(base + n * J_STEP, J_STEP), s * 3 + pair] = moved.astype(jnp.bfloat16)


GROUP = 11
PAIRS = 33


def layers(p, patches, big1, bias_big, big2, hidden, taps):
    f32 = jnp.float32

    def one(n, _):
        for u in range(GROUP):
            j = (n * GROUP + u) * 2 + EDGE - 2
            left = patches[pl.ds(j, 3)].reshape(USED, LANES)
            right = patches[pl.ds(j + 1, 3)].reshape(USED, LANES)
            before = jnp.dot(
                big1[:, :USED], jnp.concatenate([left, right], axis=1), preferred_element_type=f32
            )
            bias = bias_big[...]
            hidden[u] = jnp.maximum(before + jnp.concatenate([bias, bias], axis=1), 0.0).astype(
                jnp.bfloat16
            )
        for u in range(GROUP):
            j = (n * GROUP + u) * 2
            out = jnp.dot(big2[...], hidden[u], preferred_element_type=f32)
            taps[j] = out[:, :LANES]
            taps[j + 1] = out[:, LANES:]
        return 0

    lax.fori_loop(0, PAIRS // GROUP, one, 0)
    taps[(2 * PAIRS - 1) * p.c] = jnp.zeros((72, LANES), f32)


def finish(taps, bias2, own, other):
    step = 16
    for n in range(HALF // step):
        start = n * step
        sums = []
        for d in range(3):
            total = None
            for b in range(3):
                row = (b * 3 + d) * 8
                part = taps[start + b : start + b + step, row : row + 8]
                total = part if total is None else total + part
            sums.append(total)
        value = sums[1] + shifted(sums[0], -1) + shifted(sums[2], 1)
        value = jnp.maximum(value + bias2, 0.0)
        for i in range(2):
            own[i, start : start + step] = value[:, 2 * i : 2 * i + 2]
            other[i, start : start + step] = value[:, 4 + 2 * i : 6 + 2 * i]


def kernel(
    a_hbm, b_hbm, w1_hbm, bias1_hbm, w2_hbm, bias2_hbm,
    out_hbm,
    a_ref, b_ref, w1_ref, w2_ref, bias1_ref, bias2_ref, load_sem,
    a_rows, b_rows, a_perm, b_perm, patches, taps, big1, bias_big, big2, hidden, own, other,
    send_sem, recv_sem,
):
    p = Place(lax.axis_index("ra"), lax.axis_index("rb"))
    barrier, count = greet(p)
    pairs = (
        (a_hbm, a_ref), (b_hbm, b_ref), (w1_hbm, w1_ref),
        (w2_hbm, w2_ref), (bias1_hbm, bias1_ref), (bias2_hbm, bias2_ref),
    )
    loads = [
        pltpu.make_async_copy(src, dst, load_sem.at[n]) for n, (src, dst) in enumerate(pairs)
    ]
    for load in loads:
        load.start()
    loads[0].wait()
    a_rows[1 + p.c, p.rb] = normalized(a_ref)
    loads[1].wait()
    b_rows[1, p.c, p.x * 2 + p.zh] = normalized(b_ref)
    pl.semaphore_wait(barrier, count)

    def meanwhile():
        for load in loads[2:]:
            load.wait()
        weights(p, w1_ref, bias1_ref, w2_ref, big1, bias_big, big2)

    def have_b():
        arrange_b(p, b_rows, b_perm)

    copies = gather(p, a_rows, b_rows, send_sem, recv_sem, meanwhile, have_b)
    arrange_a(p, a_rows, a_perm)
    correlate(p, a_perm, b_perm, patches)
    layers(p, patches, big1, bias_big, big2, hidden, taps)
    finish(taps, bias2_ref[0], own, other)
    columns = pl.ds(HALF * p.c, HALF)
    handed = copies.start(other, out_hbm.at[:, columns], p.mate)
    kept = pltpu.make_async_copy(own, out_hbm.at[:, columns], load_sem.at[0])
    kept.start()
    copies.wait_send()
    kept.wait()
    handed.wait_recv()
    assert len(copies.started) <= N_COPIES, len(copies.started)


def compute_scratch(channels):
    bf16, f32 = jnp.bfloat16, jnp.float32
    return [
        pltpu.VMEM((4, 16, 16, channels), bf16),
        pltpu.VMEM((3, 2, 8, 16, channels), bf16),
        pltpu.VMEM((CHUNKS * 64, channels), bf16),
        pltpu.VMEM((6, LANES, channels), bf16),
        pltpu.VMEM((CHUNKS * 8 + EDGE, 9, 16, LANES), bf16),
        pltpu.VMEM((2 * PAIRS, 72, LANES), f32),
        pltpu.VMEM((CELLS * HID, COLS), bf16),
        pltpu.VMEM((CELLS * HID, LANES), f32),
        pltpu.VMEM((72, CELLS * HID), bf16),
        pltpu.VMEM((GROUP, CELLS * HID, 256), bf16),
        pltpu.VMEM((2, HALF, 2, LANES), f32),
        pltpu.VMEM((2, HALF, 2, LANES), f32),
    ]


def per_device(features_a, features_b, weight_one, bias_one, weight_two, bias_two):
    channels = features_a.shape[-1]
    arguments = (features_a, features_b, weight_one, bias_one, weight_two, bias_two)
    vmem = [pltpu.VMEM(v.shape, v.dtype) for v in (features_a, features_b, weight_one, weight_two)]
    smem = [pltpu.SMEM(v.shape, v.dtype) for v in (bias_one, bias_two)]
    return pl.pallas_call(
        kernel,
        out_shape=jax.ShapeDtypeStruct((2, LANES, 2, LANES), jnp.float32),
        in_specs=[pl.BlockSpec(memory_space=pl.ANY)] * 6,
        out_specs=pl.BlockSpec(memory_space=pl.ANY),
        scratch_shapes=vmem
        + smem
        + [pltpu.SemaphoreType.DMA((6,))]
        + compute_scratch(channels)
        + [pltpu.SemaphoreType.DMA((N_COPIES,)), pltpu.SemaphoreType.DMA((N_COPIES + 4,))],
        compiler_params=pltpu.CompilerParams(
            collective_id=0, has_side_effects=True, vmem_limit_bytes=60 * 1024 * 1024
        ),
        name="consensus",
    )(*arguments)


def solution(mesh):
    return jax.shard_map(
        per_device,
        mesh=mesh,
        in_specs=(P("ra", "rb", None), P("rb", "ra", None), P(), P(), P(), P()),
        out_specs=P("ra", None, "rb", None),
        check_vma=False,
    )
```

time: 708 us -> 45.6 us (0.06)
  the two profiles are of different devices: /device:TPU:232 before, /device:TPU:1 now
where the time goes in v2:
time: 45.6 us; the launch traced here: 45.4 us
  Pallas kernels  43.1 us (95%)
  local copies, waits for them, and re-layouts  1.67 us (4%)
  between operations  0.66 us (1%)
    pallas_call x1, Pallas kernels, per_device(): pl.pallas_call(kernel, out_shape=jax.ShapeDtypeStruct((2, LANES, 2, LANES...  43.1 us
    unnamed x1, local copies, waits for them, and re-layouts  1.67 us

profile of v2, /device:TPU:1, one launch (start us, length us, event | category | flops | bytes accessed | tf_op | source)
XLA Modules:
  0.0 45.4 jit_solution(889049265106323029)
XLA Ops:
  0.7 43.1 %consensus.1 = f32[2,128,2,128]{3,2,1,0:T(2,128)} custom-call(bf16[2,8,1024]{2,1,0:T(8,128)(2,1)} %a_hbm.1, bf16[2,8,1024]{2,1,0:T(8,128)(2,1)} %b_hbm.1, bf16[16,81]{1,0:T(8,128)(2,1)} %w1_hbm.1, f32[16]{0:T(128)} %bias1_hbm.1, bf16[16,81]{1,0:T(8,128)(2,1)} %w2_hbm.1, f32[1]{0:T(128)S(6)} %copy.8.bias2_hbm), custom_call_target="tpu_custom_call" | custom-call | tf_op jit(solution)/shard_map/consensus/pallas_call | solution.py:496
  43.7 1.7 %copy.9 = f32[2,128,2,128]{3,2,1,0:T(2,128)} copy(f32[2,128,2,128]{3,2,1,0:T(2,128)} %consensus.1) | data formatting | bytes 524288

commit v3 on v2

--- a/solution.py
+++ b/solution.py
@@ -42,7 +42,7 @@
 class Copies:
     def __init__(self, send_sem, recv_sem):
         self.send_sem, self.recv_sem = send_sem, recv_sem
-        self.started = []
+        self.started, self.waiting = [], []
 
     def start(self, src, dst, device, arrives=None, later=False):
         n = len(self.started)
@@ -57,15 +57,18 @@
         if later:
             return copy
         copy.start()
-        self.started.append((copy, None))
+        self.started.append(copy)
+        self.waiting.append((copy, None))
         return copy
 
     def start_when(self, copy, when):
         pl.when(when)(copy.start)
-        self.started.append((copy, when))
+        self.started.append(copy)
+        self.waiting.append((copy, when))
 
     def wait_send(self):
-        for copy, when in self.started:
+        started, self.waiting = self.waiting, []
+        for copy, when in started:
             if when is None:
                 copy.wait_send()
             else:
@@ -264,6 +267,7 @@
         for copy in arrivals:
             copy.wait_recv()
         mates_a.append(mate_a(slot, lax.rem(y + 2, 4) * 4, 4))
+    copies.wait_send()
     for copy in mates_b:
         copy.wait_recv()
     have_b()
@@ -374,7 +378,7 @@
                 patches[pl.ds(base + n * J_STEP, J_STEP), s * 3 + pair] = moved.astype(jnp.bfloat16)
 
 
-GROUP = 11
+GROUP = 33
 PAIRS = 33
 
 
@@ -419,8 +423,9 @@
         value = sums[1] + shifted(sums[0], -1) + shifted(sums[2], 1)
         value = jnp.maximum(value + bias2, 0.0)
         for i in range(2):
-            own[i, start : start + step] = value[:, 2 * i : 2 * i + 2]
-            other[i, start : start + step] = value[:, 4 + 2 * i : 6 + 2 * i]
+            rows = slice(2 * start, 2 * (start + step))
+            own[i, rows] = value[:, 2 * i : 2 * i + 2].reshape(2 * step, LANES)
+            other[i, rows] = value[:, 4 + 2 * i : 6 + 2 * i].reshape(2 * step, LANES)
 
 
 def kernel(
@@ -460,7 +465,7 @@
     correlate(p, a_perm, b_perm, patches)
     layers(p, patches, big1, bias_big, big2, hidden, taps)
     finish(taps, bias2_ref[0], own, other)
-    columns = pl.ds(HALF * p.c, HALF)
+    columns = pl.ds(2 * HALF * p.c, 2 * HALF)
     handed = copies.start(other, out_hbm.at[:, columns], p.mate)
     kept = pltpu.make_async_copy(own, out_hbm.at[:, columns], load_sem.at[0])
     kept.start()
@@ -483,8 +488,8 @@
         pltpu.VMEM((CELLS * HID, LANES), f32),
         pltpu.VMEM((72, CELLS * HID), bf16),
         pltpu.VMEM((GROUP, CELLS * HID, 256), bf16),
-        pltpu.VMEM((2, HALF, 2, LANES), f32),
-        pltpu.VMEM((2, HALF, 2, LANES), f32),
+        pltpu.VMEM((2, 2 * HALF, LANES), f32),
+        pltpu.VMEM((2, 2 * HALF, LANES), f32),
     ]
 
 
@@ -493,9 +498,9 @@
     arguments = (features_a, features_b, weight_one, bias_one, weight_two, bias_two)
     vmem = [pltpu.VMEM(v.shape, v.dtype) for v in (features_a, features_b, weight_one, weight_two)]
     smem = [pltpu.SMEM(v.shape, v.dtype) for v in (bias_one, bias_two)]
-    return pl.pallas_call(
+    rows = pl.pallas_call(
         kernel,
-        out_shape=jax.ShapeDtypeStruct((2, LANES, 2, LANES), jnp.float32),
+        out_shape=jax.ShapeDtypeStruct((2, 2 * LANES, LANES), jnp.float32),
         in_specs=[pl.BlockSpec(memory_space=pl.ANY)] * 6,
         out_specs=pl.BlockSpec(memory_space=pl.ANY),
         scratch_shapes=vmem
@@ -508,6 +513,7 @@
         ),
         name="consensus",
     )(*arguments)
+    return rows.reshape(2, LANES, 2, LANES)
 
 
 def solution(mesh):

time: 45.6 us -> 45.1 us (0.989)
  Pallas kernels: 43.1 us -> 42.5 us
    pallas_call x1, Pallas kernels: 43.1 us -> 42.5 us  [per_device(): pl.pallas_call(kernel, out_shape=jax.ShapeDtypeStruct((2, 2 * LANES, LANE...]
where the time goes in v3:
time: 45.1 us; the launch traced here: 44.9 us
  Pallas kernels  42.5 us (94%)
  local copies, waits for them, and re-layouts  1.67 us (4%)
  between operations  0.66 us (1%)
    pallas_call x1, Pallas kernels, per_device(): pl.pallas_call(kernel, out_shape=jax.ShapeDtypeStruct((2, 2 * LANES, LANE...  42.5 us
    unnamed x1, local copies, waits for them, and re-layouts  1.67 us

profile of v3, /device:TPU:1, one launch (start us, length us, event | category | flops | bytes accessed | tf_op | source)
XLA Modules:
  0.0 44.9 jit_solution(11652942942571120571)
XLA Ops:
  0.7 42.5 %consensus.1 = f32[2,256,128]{2,1,0:T(8,128)} custom-call(bf16[2,8,1024]{2,1,0:T(8,128)(2,1)} %a_hbm.1, bf16[2,8,1024]{2,1,0:T(8,128)(2,1)} %b_hbm.1, bf16[16,81]{1,0:T(8,128)(2,1)} %w1_hbm.1, f32[16]{0:T(128)} %bias1_hbm.1, bf16[16,81]{1,0:T(8,128)(2,1)} %w2_hbm.1, f32[1]{0:T(128)S(6)} %copy.8.bias2_hbm), custom_call_target="tpu_custom_call" | custom-call | tf_op jit(solution)/shard_map/consensus/pallas_call | solution.py:501
  43.2 1.7 %copy.9 = f32[2,128,2,128]{3,2,1,0:T(2,128)} copy(f32[2,128,2,128]{3,2,1,0:T(2,128)} %bitcast.1) | data formatting | bytes 524288

commit v4 on v3

--- a/solution.py
+++ b/solution.py
@@ -160,11 +160,11 @@
     here, there = x * 2 + zh, x * 2 + 1 - zh
     mates_a, mates_b = [], []
 
+    b_far = copies.start(chunk_b(1, here), chunk_b(1, here), p.far)
+    rb_own = to_rb(here)
     end = (p.outer, y * 4 + jnp.where(zl >= 2, 0, 3))
     copies.start(chunk_a(so, rb), chunk_a(3 - oo, rb), end, arrives=CHAIN + zl)
-    b_far = copies.start(chunk_b(1, here), chunk_b(1, here), p.far)
     z_own = [copies.start(chunk_a(so, rb), chunk_a(so, rb), d) for d in p.line]
-    rb_own = to_rb(here)
     y_own = [to_y(so, rb)]
     x_own = [to_x(1, here)]
 
@@ -193,17 +193,17 @@
     from_prev = [jnp.where(zl == 0, there, here), jnp.where(zl == 0, here, there)]
     from_next = [jnp.where(zl == 3, there, here), jnp.where(zl == 3, here, there)]
 
-    chain(chain_order[0])
-    line(1)
-    chain(chain_order[1])
-    line(3)
     for q, copy, index in ((0, rb_own[0], from_prev[0]), (2, rb_own[1], from_next[0])):
         copy.wait_recv()
         x_own.append(to_x(q, index))
-    line(2)
+    chain(chain_order[0])
+    line(1)
     b_far.wait_recv()
     rb_far = to_rb(there)
     x_far = [to_x(1, there)]
+    chain(chain_order[1])
+    line(3)
+    line(2)
 
     left_col = [lax.rem(y + 3, 4) * 4 + lax.rem(zl + 4 - t, 4) for t in range(4)]
     order = (0, 1, 3, 2)
@@ -215,12 +215,12 @@
         y_on.append(copies.start(chunk, chunk, p.right_y))
 
     own_on(0)
-    chain(chain_order[2])
-    chain(chain_order[3])
-    own_on(1)
     for q, copy, index in ((0, rb_far[0], from_prev[1]), (2, rb_far[1], from_next[1])):
         copy.wait_recv()
         x_far.append(to_x(q, index))
+    chain(chain_order[2])
+    own_on(1)
+    chain(chain_order[3])
     own_on(2)
     own_on(3)
 

time: 45.1 us -> 44.6 us (0.989)
    pallas_call x1, Pallas kernels: 42.5 us -> 42.1 us  [per_device(): pl.pallas_call(kernel, out_shape=jax.ShapeDtypeStruct((2, 2 * LANES, LANE...]
where the time goes in v4:
time: 44.6 us; the launch traced here: 44.4 us
  Pallas kernels  42.1 us (94%)
  local copies, waits for them, and re-layouts  1.67 us (4%)
  between operations  0.66 us (1%)
    pallas_call x1, Pallas kernels, per_device(): pl.pallas_call(kernel, out_shape=jax.ShapeDtypeStruct((2, 2 * LANES, LANE...  42.1 us
    unnamed x1, local copies, waits for them, and re-layouts  1.67 us

profile of v4, /device:TPU:1, one launch (start us, length us, event | category | flops | bytes accessed | tf_op | source)
XLA Modules:
  0.0 44.4 jit_solution(1450211790763826613)
XLA Ops:
  0.7 42.1 %consensus.1 = f32[2,256,128]{2,1,0:T(8,128)} custom-call(bf16[2,8,1024]{2,1,0:T(8,128)(2,1)} %a_hbm.1, bf16[2,8,1024]{2,1,0:T(8,128)(2,1)} %b_hbm.1, bf16[16,81]{1,0:T(8,128)(2,1)} %w1_hbm.1, f32[16]{0:T(128)} %bias1_hbm.1, bf16[16,81]{1,0:T(8,128)(2,1)} %w2_hbm.1, f32[1]{0:T(128)S(6)} %copy.8.bias2_hbm), custom_call_target="tpu_custom_call" | custom-call | tf_op jit(solution)/shard_map/consensus/pallas_call | solution.py:501
  42.7 1.7 %copy.9 = f32[2,128,2,128]{3,2,1,0:T(2,128)} copy(f32[2,128,2,128]{3,2,1,0:T(2,128)} %bitcast.1) | data formatting | bytes 524288

commit v5 on v4

--- a/solution.py
+++ b/solution.py
@@ -408,7 +408,7 @@
     taps[(2 * PAIRS - 1) * p.c] = jnp.zeros((72, LANES), f32)
 
 
-def finish(taps, bias2, own, other):
+def finish(taps, own, other):
     step = 16
     for n in range(HALF // step):
         start = n * step
@@ -421,7 +421,6 @@
                 total = part if total is None else total + part
             sums.append(total)
         value = sums[1] + shifted(sums[0], -1) + shifted(sums[2], 1)
-        value = jnp.maximum(value + bias2, 0.0)
         for i in range(2):
             rows = slice(2 * start, 2 * (start + step))
             own[i, rows] = value[:, 2 * i : 2 * i + 2].reshape(2 * step, LANES)
@@ -429,9 +428,9 @@
 
 
 def kernel(
-    a_hbm, b_hbm, w1_hbm, bias1_hbm, w2_hbm, bias2_hbm,
+    a_hbm, b_hbm, w1_hbm, bias1_hbm, w2_hbm,
     out_hbm,
-    a_ref, b_ref, w1_ref, w2_ref, bias1_ref, bias2_ref, load_sem,
+    a_ref, b_ref, w1_ref, w2_ref, bias1_ref, load_sem,
     a_rows, b_rows, a_perm, b_perm, patches, taps, big1, bias_big, big2, hidden, own, other,
     send_sem, recv_sem,
 ):
@@ -439,7 +438,7 @@
     barrier, count = greet(p)
     pairs = (
         (a_hbm, a_ref), (b_hbm, b_ref), (w1_hbm, w1_ref),
-        (w2_hbm, w2_ref), (bias1_hbm, bias1_ref), (bias2_hbm, bias2_ref),
+        (w2_hbm, w2_ref), (bias1_hbm, bias1_ref),
     )
     loads = [
         pltpu.make_async_copy(src, dst, load_sem.at[n]) for n, (src, dst) in enumerate(pairs)
@@ -464,7 +463,7 @@
     arrange_a(p, a_rows, a_perm)
     correlate(p, a_perm, b_perm, patches)
     layers(p, patches, big1, bias_big, big2, hidden, taps)
-    finish(taps, bias2_ref[0], own, other)
+    finish(taps, own, other)
     columns = pl.ds(2 * HALF * p.c, 2 * HALF)
     handed = copies.start(other, out_hbm.at[:, columns], p.mate)
     kept = pltpu.make_async_copy(own, out_hbm.at[:, columns], load_sem.at[0])
@@ -495,25 +494,25 @@
 
 def per_device(features_a, features_b, weight_one, bias_one, weight_two, bias_two):
     channels = features_a.shape[-1]
-    arguments = (features_a, features_b, weight_one, bias_one, weight_two, bias_two)
+    arguments = (features_a, features_b, weight_one, bias_one, weight_two)
     vmem = [pltpu.VMEM(v.shape, v.dtype) for v in (features_a, features_b, weight_one, weight_two)]
-    smem = [pltpu.SMEM(v.shape, v.dtype) for v in (bias_one, bias_two)]
+    smem = [pltpu.SMEM(v.shape, v.dtype) for v in (bias_one,)]
     rows = pl.pallas_call(
         kernel,
         out_shape=jax.ShapeDtypeStruct((2, 2 * LANES, LANES), jnp.float32),
-        in_specs=[pl.BlockSpec(memory_space=pl.ANY)] * 6,
+        in_specs=[pl.BlockSpec(memory_space=pl.ANY)] * 5,
         out_specs=pl.BlockSpec(memory_space=pl.ANY),
         scratch_shapes=vmem
         + smem
-        + [pltpu.SemaphoreType.DMA((6,))]
+        + [pltpu.SemaphoreType.DMA((5,))]
         + compute_scratch(channels)
         + [pltpu.SemaphoreType.DMA((N_COPIES,)), pltpu.SemaphoreType.DMA((N_COPIES + 4,))],
         compiler_params=pltpu.CompilerParams(
-            collective_id=0, has_side_effects=True, vmem_limit_bytes=60 * 1024 * 1024
+            collective_id=0, has_side_effects=True, vmem_limit_bytes=40 * 1024 * 1024
         ),
         name="consensus",
-    )(*arguments)
-    return rows.reshape(2, LANES, 2, LANES)
+    )(*[pltpu.with_memory_space_constraint(v, pltpu.HBM) for v in arguments])
+    return jax.nn.relu(rows.reshape(2, LANES, 2, LANES) + bias_two[0])
 
 
 def solution(mesh):

time: 44.6 us -> 43.5 us (0.975)
  local copies, waits for them, and re-layouts: 1.67 us -> 0 us
  other arithmetic: 0 us -> 0.72 us
    unnamed x1 -> x0, local copies, waits for them, and re-layouts: 1.67 us -> none
    max x0 -> x1, other arithmetic: none -> 0.72 us  [per_device(): return jax.nn.relu(rows.reshape(2, LANES, 2, LANES) + bias_two[0])]
where the time goes in v5:
time: 43.5 us; the launch traced here: 43.3 us
  Pallas kernels  41.9 us (96%)
  other arithmetic  0.72 us (2%)
  between operations  0.66 us (2%)
    pallas_call x1, Pallas kernels, per_device(): pl.pallas_call(kernel, out_shape=jax.ShapeDtypeStruct((2, 2 * LANES, LANE...  41.9 us

profile of v5, /device:TPU:1, one launch (start us, length us, event | category | flops | bytes accessed | tf_op | source)
XLA Modules:
  0.0 43.3 jit_solution(9913292337843515296)
XLA Ops:
  0.7 41.9 %consensus.1 = f32[2,256,128]{2,1,0:T(8,128)S(1)} custom-call(bf16[2,8,1024]{2,1,0:T(8,128)(2,1)} %a_hbm.1, bf16[2,8,1024]{2,1,0:T(8,128)(2,1)} %b_hbm.1, bf16[16,81]{1,0:T(8,128)(2,1)} %w1_hbm.1, f32[16]{0:T(128)} %bias1_hbm.1, bf16[16,81]{1,0:T(8,128)(2,1)} %w2_hbm.1), custom_call_target="tpu_custom_call" | custom-call | tf_op jit(solution)/shard_map/consensus/pallas_call | solution.py:500
  42.6 0.7 %add_maximum_fusion = f32[2,256,128]{2,1,0:T(8,128)} fusion(f32[2,256,128]{2,1,0:T(8,128)S(1)} %consensus.1, f32[]{:T(128)} %bitcast.2), kind=kLoop, calls=%fused_computation | loop fusion | flops 131072 | bytes 524292 | tf_op jit(solution)/shard_map/jit(relu)/max | solution.py:515

commit v6 on v5

--- a/solution.py
+++ b/solution.py
@@ -263,11 +263,11 @@
         copy.wait_recv()
         if n % 2 == 1:
             mates_b.append(mate_b((1, 0, 2)[n // 2], across, 2))
+    copies.wait_send()
     for slot, arrivals in ((so, y_on), (oo, outer_on)):
         for copy in arrivals:
             copy.wait_recv()
         mates_a.append(mate_a(slot, lax.rem(y + 2, 4) * 4, 4))
-    copies.wait_send()
     for copy in mates_b:
         copy.wait_recv()
     have_b()

time: 43.5 us -> 44.1 us (1.014)
  Pallas kernels: 41.9 us -> 42.6 us
    pallas_call x1, Pallas kernels: 41.9 us -> 42.6 us  [per_device(): pl.pallas_call(kernel, out_shape=jax.ShapeDtypeStruct((2, 2 * LANES, LANE...]
where the time goes in v6:
time: 44.1 us; the launch traced here: 44 us
  Pallas kernels  42.6 us (97%)
  other arithmetic  0.72 us (2%)
  between operations  0.66 us (1%)
    pallas_call x1, Pallas kernels, per_device(): pl.pallas_call(kernel, out_shape=jax.ShapeDtypeStruct((2, 2 * LANES, LANE...  42.6 us

profile of v6, /device:TPU:1, one launch (start us, length us, event | category | flops | bytes accessed | tf_op | source)
XLA Modules:
  0.0 44.0 jit_solution(7437543367300215721)
XLA Ops:
  0.7 42.6 %consensus.1 = f32[2,256,128]{2,1,0:T(8,128)S(1)} custom-call(bf16[2,8,1024]{2,1,0:T(8,128)(2,1)} %a_hbm.1, bf16[2,8,1024]{2,1,0:T(8,128)(2,1)} %b_hbm.1, bf16[16,81]{1,0:T(8,128)(2,1)} %w1_hbm.1, f32[16]{0:T(128)} %bias1_hbm.1, bf16[16,81]{1,0:T(8,128)(2,1)} %w2_hbm.1), custom_call_target="tpu_custom_call" | custom-call | tf_op jit(solution)/shard_map/consensus/pallas_call | solution.py:500
  43.3 0.7 %add_maximum_fusion = f32[2,256,128]{2,1,0:T(8,128)} fusion(f32[2,256,128]{2,1,0:T(8,128)S(1)} %consensus.1, f32[]{:T(128)} %bitcast.2), kind=kLoop, calls=%fused_computation | loop fusion | flops 131072 | bytes 524292 | tf_op jit(solution)/shard_map/jit(relu)/max | solution.py:515
